TPU v7x, 32 devices: a whole 2x2x4 slice. The times are simulated.
32 devices in a mesh: ang: 8 (over z, x), rad: 4 (over y, core).
Axes of the slice: x: 2, y: 2, z: 4, core: 2. Of those that a mesh axis runs over, the one named last changes fastest.
Arguments:
- right_side: float32 [64, 512, 256], P('rad', 'ang'), may hold values from -6 to 6
- conduct: float32 [64, 512], P('rad', 'ang'), may hold values from 0.25 to 4
- local_inverse: bfloat16 [8, 4, 1024, 1024], P('ang', 'rad'), may hold values from -1 to 3, as said below
- primal_basis: float32 [8, 4, 1024, 16], P('ang', 'rad'), may hold values from -0.22297633 to 0.22297633
- coarse_inverse: float32 [16, 16], replicated, may hold values from -1 to 3, as said below
Outputs:
- solution_field: float32 [64, 512, 256], P('rad', 'ang')
Inputs may be any that keep to these rules, and one draw needn't show every extreme that they name: `local_inverse`: each block is symmetric positive definite. `coarse_inverse`: symmetric positive definite.
All inputs are finite; a program needn't handle non-finite values.
Results may differ from a plain program's by a relative error of at most 0.0027.
Values sent between devices are 32-bit elements; how exact they have to be, the bound alone decides.
A program may use at most 64 MiB of HBM per device.

v0:
```python
import jax
import jax.numpy as jnp
from jax import lax
from jax.sharding import PartitionSpec as P

ITERS = 3


def padded(shard, sides, width, wrap):
    for axis, dim in sides:
        count, length = (lax.axis_size(axis), shard.shape[dim])
        up = [(i, (i + 1) % count) for i in range(count if wrap else count - 1)]
        down = [(j, i) for i, j in up]
        last = lax.slice_in_dim(shard, length - width, length, axis=dim)
        initial = lax.slice_in_dim(shard, 0, width, axis=dim)
        before = lax.ppermute(last, axis, up)
        after = lax.ppermute(initial, axis, down)
        shard = jnp.concatenate([before, shard, after], axis=dim)
    return shard


def operate(field, conduct):
    angular = padded(field, (("ang", 1),), 1, True)
    radial = padded(field, (("rad", 0),), 1, False)
    beside = angular[:, 2:] + angular[:, :-2] + radial[2:] + radial[:-2]
    return (4.0 + conduct)[:, :, None] * field - beside


def precondition(residual, inverse_block, basis_block, coarse_inverse):
    rows, width, cols = residual.shape
    flat = residual.reshape(rows * width, cols)
    coarse_local = jnp.dot(basis_block.T, flat, precision=lax.Precision.HIGHEST)
    local = jnp.dot(inverse_block, flat.astype(jnp.bfloat16), preferred_element_type=jnp.float32)
    coarse = lax.psum(coarse_local, ("ang", "rad"))
    coarse_z = jnp.dot(coarse_inverse, coarse, precision=lax.Precision.HIGHEST)
    zed = local + jnp.dot(basis_block, coarse_z, precision=lax.Precision.HIGHEST)
    product = lax.psum(jnp.sum(flat * zed, axis=0), ("ang", "rad"))
    return (zed.reshape(rows, width, cols), product)


def per_device(right_side, conduct, local_inverse, primal_basis, coarse_inverse):
    ncell = local_inverse.shape[2]
    kprim = primal_basis.shape[3]
    inverse_block = local_inverse.reshape(ncell, ncell)
    basis_block = primal_basis.reshape(ncell, kprim)
    solution_field = jnp.zeros_like(right_side)
    residual = right_side
    zed, product = precondition(residual, inverse_block, basis_block, coarse_inverse)
    direction = zed
    for step in range(ITERS):
        image = operate(direction, conduct)
        curve = lax.psum(jnp.sum(direction * image, axis=(0, 1)), ("ang", "rad"))
        alpha = product / curve
        solution_field = solution_field + alpha * direction
        residual = residual - alpha * image
        if step + 1 < ITERS:
            zed, fresh = precondition(residual, inverse_block, basis_block, coarse_inverse)
            ratio = fresh / product
            direction = zed + ratio * direction
            product = fresh
    return solution_field


def solution(mesh):
    return jax.shard_map(
        per_device,
        mesh=mesh,
        in_specs=(
            P("rad", "ang", None),
            P("rad", "ang"),
            P("ang", "rad", None, None),
            P("ang", "rad", None, None),
            P(),
        ),
        out_specs=P("rad", "ang", None),
        check_vma=False,
    )
```

profile of v0, /device:TPU:0, one launch (start us, length us, event | category | flops | bytes accessed | tf_op | source)
XLA Modules:
  0.0 408.0 jit_solution(12056681111804193012)
XLA Ops:
  0.0 2.2 convert_element_type.18
  3.6 42.1 %psum.63 = f32[16,256]{1,0:T(8,128)S(1)} all-reduce(f32[16,256]{1,0:T(8,128)S(1)} %fusion.28), channel_id=1, replica_groups=mesh['ang'=8,'rad'=4] {'ang','rad'}, use_global_device_ids=true, to_apply=%region_0.0 | all-reduce | flops 4096 | bytes 32768 | tf_op jit(solution)/shard_map/psum | solution.py:34
  46.1 1.8 fusion.4
  49.1 4.0 collective-permute-start
  54.4 3.0 collective-permute-start.3
  57.4 2.0 collective-permute-done.1
  59.9 40.3 %all-reduce = (f32[256]{0:T(256)S(1)}, f32[256]{0:T(256)S(1)}) all-reduce(f32[256]{0:T(256)S(1)} %get-tuple-element.23, f32[256]{0:T(256)S(1)} %multiply_reduce_fusion.3), channel_id=1, replica_groups=mesh['ang'=8,'rad'=4] {'ang','rad'}, use_global_device_ids=true, to_apply=%region_2.0 | all-reduce | flops 512 | bytes 4096 | tf_op jit(solution)/shard_map/psum | solution.py:37
  100.2 2.5 fusion.31
  103.6 1.8 convolution_bitcast_fusion.2
  105.4 2.6 copy.12
  108.0 41.2 %psum.66 = f32[16,256]{0,1:T(8,128)S(1)} all-reduce(f32[16,256]{0,1:T(8,128)S(1)} %convolution_bitcast_fusion.2), channel_id=1, replica_groups=mesh['ang'=8,'rad'=4] {'ang','rad'}, use_global_device_ids=true, to_apply=%region_5.0 | all-reduce | flops 4096 | bytes 32768 | tf_op jit(solution)/shard_map/psum | solution.py:34
  149.5 1.8 fusion.2
  151.3 2.0 fusion.7
  153.3 2.5 copy.13
  157.5 39.9 %psum.67 = f32[256]{0:T(256)S(1)} all-reduce(f32[256]{0:T(256)S(1)} %multiply_reduce_fusion.2), channel_id=1, replica_groups=mesh['ang'=8,'rad'=4] {'ang','rad'}, use_global_device_ids=true, to_apply=%region_7.0 | all-reduce | flops 256 | bytes 2048 | tf_op jit(solution)/shard_map/psum | solution.py:37
  200.2 3.0 collective-permute-start.7
  203.2 4.0 collective-permute-start.4
  208.7 5.0 %collective-permute-done.5 = f32[16,1,256]{2,1,0:T(1,128)S(1)} collective-permute-done((f32[16,1,256]{2,1,0:T(1,128)S(1)}, f32[16,1,256]{2,1,0:T(1,128)S(1)}, u32[]{:S(2)}, u32[]{:S(2)}) %collective-permute-start.5) | collective-permute-done | bytes 16416 | tf_op jit(solution)/shard_map/ppermute | solution.py:16
  214.1 37.1 %psum.68 = f32[256]{0:T(256)S(1)} all-reduce(f32[256]{0:T(256)S(1)} %multiply_reduce_fusion.1), channel_id=1, replica_groups=mesh['ang'=8,'rad'=4] {'ang','rad'}, use_global_device_ids=true, to_apply=%region_9.0 | all-reduce | flops 256 | bytes 2048 | tf_op jit(solution)/shard_map/psum | solution.py:52
  251.2 4.9 %fusion.30 = (bf16[16,64,256]{2,1,0:T(8,128)(2,1)}, f32[16,64,256]{2,1,0:T(8,128)S(1)}) fusion(f32[16,64,256]{2,1,0:T(8,128)} %copy-done.3, f32[16,64,256]{2,1,0:T(8,128)} %copy-done.4, f32[1,64,256]{2,1,0:T(8,128)S(1)} %collective-permute-done.7, f32[1,64,256]{2,1,0:T(8,128)S(1)} %collective-permute-done.6, f32[16,1,256]{2,1,0:T(1,128)S(1)} %collective-permute-done.5, ...), kind=kLoop, calls=%fused_computation.60 | loop fusion | flops 3145728 | bytes 3838976 | tf_op jit(solution)/shard_map/convert_element_type | solution.py:33
  257.1 1.8 convolution_bitcast_fusion.1
  258.9 2.6 copy.14
  261.5 42.4 %psum.69 = f32[16,256]{0,1:T(8,128)S(1)} all-reduce(f32[16,256]{0,1:T(8,128)S(1)} %convolution_bitcast_fusion.1), channel_id=1, replica_groups=mesh['ang'=8,'rad'=4] {'ang','rad'}, use_global_device_ids=true, to_apply=%region_10.0 | all-reduce | flops 4096 | bytes 32768 | tf_op jit(solution)/shard_map/psum | solution.py:34
  306.0 2.0 fusion.6
  307.9 2.5 copy.15
  312.2 39.3 %psum.70 = f32[256]{0:T(256)S(1)} all-reduce(f32[256]{0:T(256)S(1)} %multiply_reduce_fusion), channel_id=1, replica_groups=mesh['ang'=8,'rad'=4] {'ang','rad'}, use_global_device_ids=true, to_apply=%region_12.0 | all-reduce | flops 256 | bytes 2048 | tf_op jit(solution)/shard_map/psum | solution.py:37
  351.5 1.8 multiply_add_fusion.1
  354.7 3.0 collective-permute-start.11
  357.7 3.3 collective-permute-start.8
  362.5 5.0 %collective-permute-done.9 = f32[16,1,256]{2,1,0:T(1,128)S(1)} collective-permute-done((f32[16,1,256]{2,1,0:T(1,128)S(1)}, f32[16,1,256]{2,1,0:T(1,128)S(1)}, u32[]{:S(2)}, u32[]{:S(2)}) %collective-permute-start.9) | collective-permute-done | bytes 16416 | tf_op jit(solution)/shard_map/ppermute | solution.py:16
  368.0 37.1 %psum.71 = f32[256]{0:T(256)S(1)} all-reduce(f32[256]{0:T(256)S(1)} %fusion.12), channel_id=1, replica_groups=mesh['ang'=8,'rad'=4] {'ang','rad'}, use_global_device_ids=true, to_apply=%region_14.0 | all-reduce | flops 256 | bytes 2048 | tf_op jit(solution)/shard_map/psum | solution.py:52
  405.1 2.9 multiply_add_fusion
  (57 shorter events, 20.2 us)
Async XLA Ops:
  0.0 46.1 %copy-start = (bf16[1,1,1024,1024]{3,2,1,0:T(8,128)(2,1)S(1)}, bf16[1,1,1024,1024]{3,2,1,0:T(8,128)(2,1)}, u32[]{:S(2)}) copy-start(bf16[1,1,1024,1024]{3,2,1,0:T(8,128)(2,1)} %param.7) | copy-start | bytes 6291460
  0.0 2.2 copy-start.1
  0.0 45.7 %copy-start.7 = (f32[16,16]{1,0:T(8,128)S(1)}, f32[16,16]{1,0:T(8,128)}, u32[]{:S(2)}) copy-start(f32[16,16]{1,0:T(8,128)} %param.9) | copy-start | bytes 3076
  46.1 1.9 copy-start.2
  46.1 1.9 copy-start.6
  48.0 9.4 %copy-start.8 = (f32[16,64]{1,0:T(8,128)S(1)}, f32[16,64]{1,0:T(8,128)}, u32[]{:S(2)}) copy-start(f32[16,64]{1,0:T(8,128)} %param.6) | copy-start | bytes 12292
  49.1 8.3 %collective-permute-start = (f32[16,1,256]{2,1,0:T(1,128)S(1)}, f32[16,1,256]{2,1,0:T(1,128)S(1)}, u32[]{:S(2)}, u32[]{:S(2)}) collective-permute-start(f32[16,1,256]{2,1,0:T(1,128)S(1)} %get-tuple-element.19), channel_id=1, source_target_pairs={{4,0},{8,4},{12,8},{16,12},{20,16},{24,20},{28,24},{0,28},{5,1},{9... | collective-permute-start | bytes 49160 | tf_op jit(solution)/shard_map/ppermute | solution.py:17
  53.0 6.4 %collective-permute-start.1 = (f32[16,1,256]{2,1,0:T(1,128)S(1)}, f32[16,1,256]{2,1,0:T(1,128)S(1)}, u32[]{:S(2)}, u32[]{:S(2)}) collective-permute-start(f32[16,1,256]{2,1,0:T(1,128)S(1)} %get-tuple-element.20), channel_id=1, source_target_pairs={{0,4},{4,8},{8,12},{12,16},{16,20},{20,24},{24,28},{28,0},{1,5},{5... | collective-permute-start | bytes 49160 | tf_op jit(solution)/shard_map/ppermute | solution.py:16
  53.1 6.4 %collective-permute-start.2 = (f32[1,64,256]{2,1,0:T(8,128)S(1)}, f32[1,64,256]{2,1,0:T(8,128)S(1)}, u32[]{:S(2)}, u32[]{:S(2)}) collective-permute-start(f32[1,64,256]{2,1,0:T(8,128)S(1)} %get-tuple-element.21), channel_id=1, source_target_pairs={{1,0},{2,1},{3,2},{5,4},{6,5},{7,6},{9,8},{10,9},{11,10},{13,12},{... | collective-permute-start | bytes 196616 | tf_op jit(solution)/shard_map/ppermute | solution.py:17
  54.4 5.1 %collective-permute-start.3 = (f32[1,64,256]{2,1,0:T(8,128)S(1)}, f32[1,64,256]{2,1,0:T(8,128)S(1)}, u32[]{:S(2)}, u32[]{:S(2)}) collective-permute-start(f32[1,64,256]{2,1,0:T(8,128)S(1)} %get-tuple-element.22), channel_id=1, source_target_pairs={{0,1},{1,2},{2,3},{4,5},{5,6},{6,7},{8,9},{9,10},{10,11},{12,13},{... | collective-permute-start | bytes 196616 | tf_op jit(solution)/shard_map/ppermute | solution.py:16
  102.6 1.0 copy-start.3
  198.8 14.8 %copy-start.4 = (f32[16,64,256]{2,1,0:T(8,128)}, f32[16,64,256]{2,1,0:T(8,128)S(1)}, u32[]{:S(2)}) copy-start(f32[16,64,256]{2,1,0:T(8,128)S(1)} %multiply_add_fusion.2) | copy-start | bytes 3145732
  198.9 14.8 %collective-permute-start.6 = (f32[1,64,256]{2,1,0:T(8,128)S(1)}, f32[1,64,256]{2,1,0:T(8,128)S(1)}, u32[]{:S(2)}, u32[]{:S(2)}) collective-permute-start(f32[1,64,256]{2,1,0:T(8,128)S(1)} %get-tuple-element.17), channel_id=1, source_target_pairs={{1,0},{2,1},{3,2},{5,4},{6,5},{7,6},{9,8},{10,9},{11,10},{13,12},{... | collective-permute-start | bytes 196616 | tf_op jit(solution)/shard_map/ppermute | solution.py:17
  200.2 13.5 %collective-permute-start.7 = (f32[1,64,256]{2,1,0:T(8,128)S(1)}, f32[1,64,256]{2,1,0:T(8,128)S(1)}, u32[]{:S(2)}, u32[]{:S(2)}) collective-permute-start(f32[1,64,256]{2,1,0:T(8,128)S(1)} %get-tuple-element.18), channel_id=1, source_target_pairs={{0,1},{1,2},{2,3},{4,5},{5,6},{6,7},{8,9},{9,10},{10,11},{12,13},{... | collective-permute-start | bytes 196616 | tf_op jit(solution)/shard_map/ppermute | solution.py:16
  203.2 5.4 %collective-permute-start.4 = (f32[16,1,256]{2,1,0:T(1,128)S(1)}, f32[16,1,256]{2,1,0:T(1,128)S(1)}, u32[]{:S(2)}, u32[]{:S(2)}) collective-permute-start(f32[16,1,256]{2,1,0:T(1,128)S(1)} %get-tuple-element.15), channel_id=1, source_target_pairs={{4,0},{8,4},{12,8},{16,12},{20,16},{24,20},{28,24},{0,28},{5,1},{9... | collective-permute-start | bytes 49160 | tf_op jit(solution)/shard_map/ppermute | solution.py:17
  207.2 6.4 %collective-permute-start.5 = (f32[16,1,256]{2,1,0:T(1,128)S(1)}, f32[16,1,256]{2,1,0:T(1,128)S(1)}, u32[]{:S(2)}, u32[]{:S(2)}) collective-permute-start(f32[16,1,256]{2,1,0:T(1,128)S(1)} %get-tuple-element.16), channel_id=1, source_target_pairs={{0,4},{4,8},{8,12},{12,16},{16,20},{20,24},{24,28},{28,0},{1,5},{5... | collective-permute-start | bytes 49160 | tf_op jit(solution)/shard_map/ppermute | solution.py:16
  256.1 1.0 copy-start.5
  353.4 14.1 %collective-permute-start.10 = (f32[1,64,256]{2,1,0:T(8,128)S(1)}, f32[1,64,256]{2,1,0:T(8,128)S(1)}, u32[]{:S(2)}, u32[]{:S(2)}) collective-permute-start(f32[1,64,256]{2,1,0:T(8,128)S(1)} %get-tuple-element.13), channel_id=1, source_target_pairs={{1,0},{2,1},{3,2},{5,4},{6,5},{7,6},{9,8},{10,9},{11,10},{13,12},{... | collective-permute-start | bytes 196616 | tf_op jit(solution)/shard_map/ppermute | solution.py:17
  354.7 12.8 %collective-permute-start.11 = (f32[1,64,256]{2,1,0:T(8,128)S(1)}, f32[1,64,256]{2,1,0:T(8,128)S(1)}, u32[]{:S(2)}, u32[]{:S(2)}) collective-permute-start(f32[1,64,256]{2,1,0:T(8,128)S(1)} %get-tuple-element.14), channel_id=1, source_target_pairs={{0,1},{1,2},{2,3},{4,5},{5,6},{6,7},{8,9},{9,10},{10,11},{12,13},{... | collective-permute-start | bytes 196616 | tf_op jit(solution)/shard_map/ppermute | solution.py:16
  357.7 4.8 %collective-permute-start.8 = (f32[16,1,256]{2,1,0:T(1,128)S(1)}, f32[16,1,256]{2,1,0:T(1,128)S(1)}, u32[]{:S(2)}, u32[]{:S(2)}) collective-permute-start(f32[16,1,256]{2,1,0:T(1,128)S(1)} %get-tuple-element.11), channel_id=1, source_target_pairs={{4,0},{8,4},{12,8},{16,12},{20,16},{24,20},{28,24},{0,28},{5,1},{9... | collective-permute-start | bytes 49160 | tf_op jit(solution)/shard_map/ppermute | solution.py:17
  361.1 6.4 %collective-permute-start.9 = (f32[16,1,256]{2,1,0:T(1,128)S(1)}, f32[16,1,256]{2,1,0:T(1,128)S(1)}, u32[]{:S(2)}, u32[]{:S(2)}) collective-permute-start(f32[16,1,256]{2,1,0:T(1,128)S(1)} %get-tuple-element.12), channel_id=1, source_target_pairs={{0,4},{4,8},{8,12},{12,16},{16,20},{20,24},{24,28},{28,0},{1,5},{5... | collective-permute-start | bytes 49160 | tf_op jit(solution)/shard_map/ppermute | solution.py:16
where the time goes:
time: 410 us; the launch traced here: 408 us
  blocking collectives  319 us (78%)
  starting transfers between devices  24.2 us (6%)
  other arithmetic  20.5 us (5%)
  matrix products  16.3 us (4%)
  waiting for transfers between devices  14.9 us (4%)
  local copies, waits for them, and re-layouts  12.4 us (3%)
    psum x3, blocking collectives, precondition(): coarse = lax.psum(coarse_local, ('ang', 'rad'))  126 us
    psum x3, blocking collectives, precondition(): product = lax.psum(jnp.sum(flat * zed, axis=0), ('ang', 'rad'))  119 us
    psum x2, blocking collectives, per_device(): curve = lax.psum(jnp.sum(direction * image, axis=(0, 1)), ('ang', 'rad'))  74.2 us
    ppermute x6, starting transfers between devices, padded(): after = lax.ppermute(initial, axis, down)  15.1 us
    ppermute x6, waiting for transfers between devices, padded(): before = lax.ppermute(last, axis, up)  12 us
    convert_element_type x3, other arithmetic, precondition(): flat.astype(jnp.bfloat16)  9.59 us
    ppermute x6, starting transfers between devices, padded(): before = lax.ppermute(last, axis, up)  9.11 us
  transfers between devices with their start and end apart: 12, of which 5 were waited for; matrix products, arithmetic and copies ran while one was open for 0% of the time, Pallas kernels for 0%

commit v1 on v0

v1 whole, which is shorter than its diff:
```python
import functools
import jax
import jax.numpy as jnp
from jax import lax
from jax.experimental import pallas as pl
from jax.experimental.pallas import tpu as pltpu
from jax.sharding import PartitionSpec as P

ITERS = 3
F32 = jnp.float32
BF16 = jnp.bfloat16
MESH = pl.DeviceIdType.MESH


def stage_radices(n_ang):
    first = 2 if n_ang % 2 == 0 else 1
    radices, rest = [], n_ang // first
    while rest > 1:
        factor = 4 if rest % 4 == 0 else next(f for f in range(2, rest + 1) if rest % f == 0)
        radices.append(factor)
        rest //= factor
    return first, radices


def split(value):
    high = value.astype(BF16)
    return high, (value - high.astype(F32)).astype(BF16)


def kernel(dims, rhs_hbm, cond_hbm, inv_hbm, basis_hbm, coarse_hbm, out_ref,
           lx, rhs, right, image, zed, direction, diag, cond, coarse_inv,
           basis, lift, ybufs, edges, pack, *rest):
    n_ang, n_rad, lr, la, cols, kprim, first, radices = dims
    nst = 1 + len(radices)
    recvs = rest[:nst]
    (load_sem, basis_send, basis_recv, edge_send, edge_recv) = rest[nst:nst + 5]
    ar_sems = rest[nst + 5:]
    ncell = lr * la
    main, bottom = la, la + ncell
    left, rightside = bottom + la, bottom + la + lr
    total = rightside + lr

    ang, rad = lax.axis_index("ang"), lax.axis_index("rad")
    ang_up, ang_down = lax.rem(ang + 1, n_ang), lax.rem(ang + n_ang - 1, n_ang)

    loads = [
        pltpu.make_async_copy(basis_hbm, basis.at[pl.ds(main, ncell)], load_sem.at[0]),
        pltpu.make_async_copy(rhs_hbm, rhs, load_sem.at[1]),
        pltpu.make_async_copy(inv_hbm, lx.at[pl.ds(0, ncell)], load_sem.at[2]),
        pltpu.make_async_copy(cond_hbm, cond, load_sem.at[3]),
        pltpu.make_async_copy(coarse_hbm, coarse_inv, load_sem.at[4]),
    ]
    for load in loads:
        load.start()

    def partners(stage):
        found = []
        if stage == 0:
            size = n_rad * first
            low = lax.rem(ang, first)
            rank = rad * first + low
            for o in range(1, size):
                other = lax.rem(rank + o, size)
                found.append((ang - low + lax.rem(other, first), other // first))
        else:
            stride = first
            for f in radices[:stage - 1]:
                stride *= f
            f = radices[stage - 1]
            digit = lax.rem(ang // stride, f)
            for o in range(1, f):
                other = lax.rem(digit + o, f)
                found.append((ang + (other - digit) * stride, rad))
        return found

    basis[pl.ds(0, la)] = jnp.zeros((la, kprim), F32)
    basis[pl.ds(bottom, la)] = jnp.zeros((la, kprim), F32)
    for k in range(ITERS):
        ybufs[k, pl.ds(0, la)] = jnp.zeros((la, cols), F32)
        ybufs[k, pl.ds(bottom, la)] = jnp.zeros((la, cols), F32)

    groups = [partners(s) for s in range(nst)]
    barrier = pltpu.get_barrier_semaphore()
    greeted = [p for g in groups for p in g] + [(ang_up, rad), (ang_down, rad)]
    for peer in greeted:
        pl.semaphore_signal(barrier, inc=1, device_id=peer, device_id_type=MESH)

    def gather_edges(src, dst):
        for r in range(lr):
            dst[0, pl.ds(r, 1)] = src[pl.ds(main + r * la, 1)]
            dst[1, pl.ds(r, 1)] = src[pl.ds(main + r * la + la - 1, 1)]

    def exchange(buf, edge, send, recv):
        def remote(src, dst, i, peer):
            return pltpu.make_async_remote_copy(
                src_ref=src, dst_ref=dst, send_sem=send.at[i], recv_sem=recv.at[i],
                device_id=peer, device_id_type=MESH)
        upward = remote(buf.at[pl.ds(bottom - la, la)], buf.at[pl.ds(0, la)], 0, (ang, rad + 1))
        downward = remote(buf.at[pl.ds(main, la)], buf.at[pl.ds(bottom, la)], 1, (ang, rad - 1))
        ahead = remote(edge.at[1], buf.at[pl.ds(left, lr)], 2, (ang_up, rad))
        behind = remote(edge.at[0], buf.at[pl.ds(rightside, lr)], 3, (ang_down, rad))
        return upward, downward, ahead, behind

    def start_exchange(copies):
        upward, downward, ahead, behind = copies
        pl.when(rad < n_rad - 1)(upward.start)
        pl.when(rad > 0)(downward.start)
        ahead.start()
        behind.start()

    def finish_exchange(copies):
        upward, downward, ahead, behind = copies
        pl.when(rad > 0)(upward.wait_recv)
        pl.when(rad < n_rad - 1)(downward.wait_recv)
        ahead.wait_recv()
        behind.wait_recv()
        pl.when(rad < n_rad - 1)(upward.wait_send)
        pl.when(rad > 0)(downward.wait_send)
        ahead.wait_send()
        behind.wait_send()

    def reduce(phase, rows, value):
        pack[phase, 0, pl.ds(0, rows)] = value
        for stage in range(nst):
            send, recv = ar_sems[2 * stage], ar_sems[2 * stage + 1]
            copies = []
            for o, peer in enumerate(groups[stage]):
                copies.append(pltpu.make_async_remote_copy(
                    src_ref=pack.at[phase, stage, pl.ds(0, rows)],
                    dst_ref=recvs[stage].at[phase, o, pl.ds(0, rows)],
                    send_sem=send.at[phase, o], recv_sem=recv.at[phase, o],
                    device_id=peer, device_id_type=MESH))
            for copy in copies:
                copy.start()
            acc = value
            for o, copy in enumerate(copies):
                copy.wait_recv()
                acc = acc + recvs[stage][phase, o, pl.ds(0, rows)]
            value = acc
            if stage + 1 < nst:
                pack[phase, stage + 1, pl.ds(0, rows)] = value
            pending.extend(copies)
        return value

    pending = []

    loads[0].wait()
    gather_edges(basis, basis_edge := rest[-1])
    pl.semaphore_wait(barrier, len(greeted))
    basis_copies = exchange(basis, basis_edge, basis_send, basis_recv)
    start_exchange(basis_copies)

    row16 = lax.broadcasted_iota(jnp.int32, (kprim, 3 * kprim), 0)
    col48 = lax.broadcasted_iota(jnp.int32, (kprim, 3 * kprim), 1)
    pick_high = jnp.logical_or(col48 == row16, col48 == row16 + 2 * kprim).astype(F32).astype(BF16)
    pick_low = (col48 == row16 + kprim).astype(F32).astype(BF16)

    def make_lift(start, size):
        high, low = split(basis[pl.ds(start, size)])
        both = (jnp.dot(high, pick_high, preferred_element_type=F32)
                + jnp.dot(low, pick_low, preferred_element_type=F32))
        lift[pl.ds(start, size)] = both.astype(BF16)

    make_lift(main, ncell)
    row32 = lax.broadcasted_iota(jnp.int32, (2 * kprim, 3 * kprim), 0)
    col32 = lax.broadcasted_iota(jnp.int32, (2 * kprim, 3 * kprim), 1)
    flip = (row32 == col32).astype(F32).astype(BF16)
    lx[pl.ds(ncell, 2 * kprim)] = lax.dot_general(
        flip, lift[pl.ds(main, ncell)], (((1,), (1,)), ((), ())),
        preferred_element_type=F32).astype(BF16)

    loads[3].wait()
    loads[4].wait()
    eye = (lax.broadcasted_iota(jnp.int32, (la, la), 0) == lax.broadcasted_iota(jnp.int32, (la, la), 1))
    for r in range(lr):
        column = jnp.sum(jnp.where(eye, cond[pl.ds(r, 1)], 0.0), axis=1, keepdims=True)
        diag[pl.ds(r * la, la)] = jnp.broadcast_to(4.0 + column, (la, 128))

    def store_split(start, value):
        high, low = split(value)
        right[pl.ds(start, la), pl.ds(0, cols)] = high
        right[pl.ds(start, la), pl.ds(cols, cols)] = low

    tile = 256 if ncell % 256 == 0 else la

    def apply_local(vec, out):
        def body(i, acc):
            start = pl.multiple_of(i * tile, tile)
            prod = jnp.dot(lx[pl.ds(start, tile)], right[...], preferred_element_type=F32)
            got = prod[:, :cols] + prod[:, cols:]
            out[pl.ds(main + start, tile)] = got
            part = got * vec[pl.ds(start, tile)]
            return acc + jnp.sum(part.reshape(tile // 8, 8, cols), axis=0)
        acc = lax.fori_loop(0, ncell // tile, body, jnp.zeros((8, cols), F32))
        small = jnp.dot(lx[pl.ds(ncell, 2 * kprim)], right[...], preferred_element_type=F32)
        both = small[:, :cols] + small[:, cols:]
        return jnp.sum(acc, axis=0, keepdims=True), both[:kprim] + both[kprim:]

    def lifted_weights(coarse):
        weights = jnp.dot(coarse_inv[...], coarse, precision=lax.Precision.HIGHEST, preferred_element_type=F32)
        high, low = split(weights)
        energy = jnp.sum(coarse * weights, axis=0, keepdims=True)
        return jnp.concatenate([high, high, low], axis=0), energy

    step_rows = 2 * lr if total % (2 * lr) == 0 else 16
    loads[1].wait()

    def split_rhs(r, carry):
        start = pl.multiple_of(r * la, la)
        store_split(start, rhs[pl.ds(start, la)])
        return carry
    lax.fori_loop(0, lr, split_rhs, 0)
    loads[2].wait()

    rows_in = lax.broadcasted_iota(jnp.int32, (la, cols), 0)

    def apply_operator():
        def body(r, acc):
            at = pl.multiple_of(r * la, la)
            here = direction[pl.ds(at + la, la)]
            radial = direction[pl.ds(at, la)] + direction[pl.ds(at + 2 * la, la)]
            before = jnp.where(rows_in == 0, direction[pl.ds(left + r, 1)], pltpu.roll(here, 1, 0))
            after = jnp.where(rows_in == la - 1, direction[pl.ds(rightside + r, 1)], pltpu.roll(here, la - 1, 0))
            weight = diag[pl.ds(at, la)]
            weight = jnp.concatenate([weight] * (cols // 128), axis=1)
            got = weight * here - ((before + after) + radial)
            image[pl.ds(at, la)] = got
            store_split(at, got)
            return acc + jnp.sum((got * here).reshape(la // 8, 8, cols), axis=0)
        acc = lax.fori_loop(0, lr, body, jnp.zeros((8, cols), F32))
        return jnp.sum(acc, axis=0, keepdims=True)

    product = None
    alpha = None
    for k in range(ITERS):
        ybuf = ybufs.at[k]
        if k == 0:
            inner, coarse = apply_local(rhs, ybuf)
            curve = jnp.zeros((1, cols), F32)
        else:
            inner, coarse = apply_local(image, ybuf)
        edge = edges.at[k]
        gather_edges(ybuf, edge)
        copies = exchange(ybuf, edge, edge_send.at[k], edge_recv.at[k])
        start_exchange(copies)
        value = jnp.concatenate(
            [coarse, inner, curve, jnp.zeros((6, cols), F32)], axis=0)
        value = reduce(k, kprim + 8, value)
        coarse, inner, curve = value[:kprim], value[kprim:kprim + 1], value[kprim + 1:kprim + 2]
        weights, energy = lifted_weights(coarse)
        inner = inner + energy
        if k == 0:
            finish_exchange(basis_copies)
            make_lift(0, la)
            make_lift(bottom, total - bottom)
        finish_exchange(copies)
        if k == 0:
            product = inner

            def begin(i, carry):
                at = pl.multiple_of(i * step_rows, step_rows)
                got = ybuf[pl.ds(at, step_rows)] + jnp.dot(
                    lift[pl.ds(at, step_rows)], weights, preferred_element_type=F32)
                zed[pl.ds(at, step_rows)] = got
                direction[pl.ds(at, step_rows)] = got
                return carry
            lax.fori_loop(0, total // step_rows, begin, 0)
        else:
            alpha = product / curve
            fresh = alpha * alpha * inner - product
            ratio = fresh / product
            product = fresh

            def update(i, carry):
                at = pl.multiple_of(i * step_rows, step_rows)
                got = ybuf[pl.ds(at, step_rows)] + jnp.dot(
                    lift[pl.ds(at, step_rows)], weights, preferred_element_type=F32)
                fresh_zed = zed[pl.ds(at, step_rows)] - alpha * got
                zed[pl.ds(at, step_rows)] = fresh_zed
                old = direction[pl.ds(at, step_rows)]
                moved = alpha * old
                if k > 1:
                    moved = moved + solution_acc[pl.ds(at, step_rows)]
                solution_acc[pl.ds(at, step_rows)] = moved
                direction[pl.ds(at, step_rows)] = fresh_zed + ratio * old
                return carry
            solution_acc = rest[-2]
            lax.fori_loop(0, total // step_rows, update, 0)
        curve = apply_operator()
    curve = reduce(ITERS, 8, jnp.broadcast_to(curve, (8, cols)))[:1]
    alpha = product / curve

    def finish(r, carry):
        at = pl.multiple_of(r * la, la)
        out_ref[pl.ds(at, la)] = solution_acc[pl.ds(at + la, la)] + alpha * direction[pl.ds(at + la, la)]
        return carry
    lax.fori_loop(0, lr, finish, 0)
    for copy in pending:
        copy.wait_send()


def per_device(n_ang, n_rad, right_side, conduct, local_inverse, primal_basis, coarse_inverse):
    lr, la, cols = right_side.shape
    ncell, kprim = primal_basis.shape[2:]
    first, radices = stage_radices(n_ang)
    sizes = [n_rad * first] + radices
    nst = len(sizes)
    total = ncell + 2 * la + 2 * lr
    rows = kprim + 8
    dma = pltpu.SemaphoreType.DMA
    scratch = [
        pltpu.VMEM((ncell + 2 * kprim, ncell), BF16),
        pltpu.VMEM((ncell, cols), F32),
        pltpu.VMEM((ncell, 2 * cols), BF16),
        pltpu.VMEM((ncell, cols), F32),
        pltpu.VMEM((total, cols), F32),
        pltpu.VMEM((total, cols), F32),
        pltpu.VMEM((ncell, 128), F32),
        pltpu.VMEM((lr, la), F32),
        pltpu.VMEM((kprim, kprim), F32),
        pltpu.VMEM((total, kprim), F32),
        pltpu.VMEM((total, 3 * kprim), BF16),
        pltpu.VMEM((ITERS, total, cols), F32),
        pltpu.VMEM((ITERS, 2, lr, cols), F32),
        pltpu.VMEM((ITERS + 1, nst, rows, cols), F32),
    ]
    scratch += [pltpu.VMEM((ITERS + 1, s - 1, rows, cols), F32) for s in sizes]
    scratch += [dma((5,)), dma((4,)), dma((4,)), dma((ITERS, 4)), dma((ITERS, 4))]
    for s in sizes:
        scratch += [dma((ITERS + 1, s - 1)), dma((ITERS + 1, s - 1))]
    scratch += [pltpu.VMEM((total, cols), F32), pltpu.VMEM((2, lr, kprim), F32)]
    flat = pl.pallas_call(
        functools.partial(kernel, (n_ang, n_rad, lr, la, cols, kprim, first, radices)),
        out_shape=jax.ShapeDtypeStruct((ncell, cols), F32),
        in_specs=[pl.BlockSpec(memory_space=pl.ANY)] * 5,
        out_specs=pl.BlockSpec(memory_space=pltpu.VMEM),
        scratch_shapes=scratch,
        compiler_params=pltpu.CompilerParams(
            collective_id=0, has_side_effects=True, vmem_limit_bytes=48 * 1024 * 1024),
        cost_estimate=pl.CostEstimate(
            flops=2 * ITERS * ncell * ncell * 2 * cols, bytes_accessed=5 * 1024 * 1024, transcendentals=0),
    )(right_side.reshape(ncell, cols), conduct, local_inverse.reshape(ncell, ncell),
      primal_basis.reshape(ncell, kprim), coarse_inverse)
    return flat.reshape(lr, la, cols)


def solution(mesh):
    return jax.shard_map(
        functools.partial(per_device, mesh.shape["ang"], mesh.shape["rad"]),
        mesh=mesh,
        in_specs=(
            P("rad", "ang", None),
            P("rad", "ang"),
            P("ang", "rad", None, None),
            P("ang", "rad", None, None),
            P(),
        ),
        out_specs=P("rad", "ang", None),
        check_vma=False,
    )
```

time: 410 us -> 69.7 us (0.17)
  blocking collectives: 319 us -> 0 us
  Pallas kernels: 0 us -> 63.1 us
  starting transfers between devices: 24.2 us -> 0 us
  other arithmetic: 20.5 us -> 0 us
  matrix products: 16.3 us -> 0 us
  waiting for transfers between devices: 14.9 us -> 0 us
  local copies, waits for them, and re-layouts: 12.4 us -> 6.21 us
    psum x8 -> x0, blocking collectives: 319 us -> none  [the longest x3 126 us: precondition(): coarse = lax.psum(coarse_local, ('ang', 'rad'))]
    pallas_call x0 -> x1, Pallas kernels: none -> 63.1 us  [per_device(): pl.pallas_call(functools.partial(kernel, (n_ang, n_rad, lr, la, cols, kpr...]
    ppermute x12 -> x0, starting transfers between devices: 24.2 us -> none  [the longest x6 15.1 us: padded(): after = lax.ppermute(initial, axis, down)]
    dot_general x12 -> x0, matrix products: 16.3 us -> none  [the longest x3 5.43 us: precondition(): jnp.dot(inverse_block, flat.astype(jnp.bfloat16), preferred_element_type=...]
    ppermute x12 -> x0, waiting for transfers between devices: 14.9 us -> none  [the longest x6 12 us: padded(): before = lax.ppermute(last, axis, up)]
    convert_element_type x3 -> x0, other arithmetic: 9.59 us -> none  [precondition(): flat.astype(jnp.bfloat16)]
    add x4 -> x0, other arithmetic: 6.07 us -> none  [the longest x2 3.2 us: per_device(): direction = zed + ratio * direction]
    reshape x2 -> x0, local copies, waits for them, and re-layouts: 5.19 us -> none  [precondition(): flat = residual.reshape(rows * width, cols)]
  transfers between devices with their start and end apart: 12 -> 0, of which waited for: 5 -> 0; matrix products, arithmetic and copies ran while one was open for 0% -> 0% of each run, Pallas kernels for 0% -> 0%
where the time goes in v1:
time: 69.7 us; the launch traced here: 69.4 us
  Pallas kernels  63.1 us (91%)
  local copies, waits for them, and re-layouts  6.21 us (9%)
    pallas_call x1, Pallas kernels, per_device(): pl.pallas_call(functools.partial(kernel, (n_ang, n_rad, lr, la, cols, kpr...  63.1 us
    unnamed x10, local copies, waits for them, and re-layouts  6.21 us

profile of v1, /device:TPU:0, one launch (start us, length us, event | category | flops | bytes accessed | tf_op | source)
XLA Modules:
  0.0 69.4 jit_solution(14707018343035607054)
XLA Ops:
  0.0 1.0 %copy.6 = f32[1,1,1024,16]{3,2,1,0:T(8,128)S(1)} copy(f32[1,1,1024,16]{2,3,1,0:T(8,128)} %param.8) | data formatting | bytes 131072 | tf_op args[3]
  1.0 0.0 copy-start
  1.1 1.6 %copy-done = bf16[1,1,1024,1024]{3,2,1,0:T(8,128)(2,1)S(1)} copy-done((bf16[1,1,1024,1024]{3,2,1,0:T(8,128)(2,1)S(1)}, bf16[1,1,1024,1024]{3,2,1,0:T(8,128)(2,1)}, u32[]{:S(2)}) %copy-start) | copy-done | bytes 2097176
  2.6 0.0 copy-start.1
  2.6 1.2 %copy-done.1 = f32[16,64,256]{2,1,0:T(8,128)S(1)} copy-done((f32[16,64,256]{2,1,0:T(8,128)S(1)}, f32[16,64,256]{2,1,0:T(8,128)}, u32[]{:S(2)}) %copy-start.1) | copy-done | bytes 1048600
  3.9 0.0 copy-start.2
  3.9 0.7 %copy-done.2 = f32[16,64]{1,0:T(8,128)S(1)} copy-done((f32[16,64]{1,0:T(8,128)S(1)}, f32[16,64]{1,0:T(8,128)}, u32[]{:S(2)}) %copy-start.2) | copy-done | bytes 4120
  4.6 0.0 copy-start.3
  4.6 0.7 %copy-done.3 = f32[16,16]{1,0:T(8,128)S(1)} copy-done((f32[16,16]{1,0:T(8,128)S(1)}, f32[16,16]{1,0:T(8,128)}, u32[]{:S(2)}) %copy-start.3) | copy-done | bytes 1048
  5.3 63.1 %shard_map.55 = f32[1024,256]{1,0:T(8,128)S(1)} custom-call(f32[1024,256]{1,0:T(8,128)S(1)} %bitcast.7, f32[16,64]{1,0:T(8,128)S(1)} %copy-done.2, bf16[1024,1024]{1,0:T(8,128)(2,1)S(1)} %bitcast.6, f32[1024,16]{1,0:T(8,128)S(1)} %bitcast.5, f32[16,16]{1,0:T(8,128)S(1)} %copy-done.3), custom_call_target="tpu_custom_call" | custom-call | flops 3221225472 | bytes 5242880 | tf_op jit(solution)/shard_map/pallas_call | solution.py:332
  68.4 1.0 %copy.8 = f32[16,64,256]{2,1,0:T(8,128)} copy(f32[16,64,256]{2,1,0:T(8,128)S(1)} %bitcast.4) | data formatting | bytes 2097152
Async XLA Ops:
  1.0 1.6 %copy-start = (bf16[1,1,1024,1024]{3,2,1,0:T(8,128)(2,1)S(1)}, bf16[1,1,1024,1024]{3,2,1,0:T(8,128)(2,1)}, u32[]{:S(2)}) copy-start(bf16[1,1,1024,1024]{3,2,1,0:T(8,128)(2,1)} %param.7) | copy-start | bytes 6291460
  2.6 1.2 %copy-start.1 = (f32[16,64,256]{2,1,0:T(8,128)S(1)}, f32[16,64,256]{2,1,0:T(8,128)}, u32[]{:S(2)}) copy-start(f32[16,64,256]{2,1,0:T(8,128)} %param.5) | copy-start | bytes 3145732
  3.9 0.7 %copy-start.2 = (f32[16,64]{1,0:T(8,128)S(1)}, f32[16,64]{1,0:T(8,128)}, u32[]{:S(2)}) copy-start(f32[16,64]{1,0:T(8,128)} %cond_hbm.1) | copy-start | bytes 12292
  4.6 0.7 %copy-start.3 = (f32[16,16]{1,0:T(8,128)S(1)}, f32[16,16]{1,0:T(8,128)}, u32[]{:S(2)}) copy-start(f32[16,16]{1,0:T(8,128)} %coarse_hbm.1) | copy-start | bytes 3076

commit v2 on v1

--- a/solution.py
+++ b/solution.py
@@ -29,7 +29,7 @@
 
 def kernel(dims, rhs_hbm, cond_hbm, inv_hbm, basis_hbm, coarse_hbm, out_ref,
            lx, rhs, right, image, zed, direction, diag, cond, coarse_inv,
-           basis, lift, ybufs, edges, pack, *rest):
+           basis_t, basis, lift, ybufs, edges, pack, *rest):
     n_ang, n_rad, lr, la, cols, kprim, first, radices = dims
     nst = 1 + len(radices)
     recvs = rest[:nst]
@@ -38,13 +38,14 @@
     ncell = lr * la
     main, bottom = la, la + ncell
     left, rightside = bottom + la, bottom + la + lr
-    total = rightside + lr
+    total = zed.shape[0]
+    step_rows = total // (total // 256)
 
     ang, rad = lax.axis_index("ang"), lax.axis_index("rad")
     ang_up, ang_down = lax.rem(ang + 1, n_ang), lax.rem(ang + n_ang - 1, n_ang)
 
     loads = [
-        pltpu.make_async_copy(basis_hbm, basis.at[pl.ds(main, ncell)], load_sem.at[0]),
+        pltpu.make_async_copy(basis_hbm, basis_t, load_sem.at[0]),
         pltpu.make_async_copy(rhs_hbm, rhs, load_sem.at[1]),
         pltpu.make_async_copy(inv_hbm, lx.at[pl.ds(0, ncell)], load_sem.at[2]),
         pltpu.make_async_copy(cond_hbm, cond, load_sem.at[3]),
@@ -73,11 +74,11 @@
                 found.append((ang + (other - digit) * stride, rad))
         return found
 
-    basis[pl.ds(0, la)] = jnp.zeros((la, kprim), F32)
-    basis[pl.ds(bottom, la)] = jnp.zeros((la, kprim), F32)
+    basis[pl.ds(0, la)] = jnp.zeros((la, 3 * kprim), F32)
+    basis[pl.ds(bottom, total - bottom)] = jnp.zeros((total - bottom, 3 * kprim), F32)
     for k in range(ITERS):
         ybufs[k, pl.ds(0, la)] = jnp.zeros((la, cols), F32)
-        ybufs[k, pl.ds(bottom, la)] = jnp.zeros((la, cols), F32)
+        ybufs[k, pl.ds(bottom, total - bottom)] = jnp.zeros((total - bottom, cols), F32)
 
     groups = [partners(s) for s in range(nst)]
     barrier = pltpu.get_barrier_semaphore()
@@ -119,7 +120,7 @@
         ahead.wait_send()
         behind.wait_send()
 
-    def reduce(phase, rows, value):
+    def reduce(phase, rows, value, shadow=None):
         pack[phase, 0, pl.ds(0, rows)] = value
         for stage in range(nst):
             send, recv = ar_sems[2 * stage], ar_sems[2 * stage + 1]
@@ -132,6 +133,8 @@
                     device_id=peer, device_id_type=MESH))
             for copy in copies:
                 copy.start()
+            if stage == 0 and shadow is not None:
+                shadow()
             acc = value
             for o, copy in enumerate(copies):
                 copy.wait_recv()
@@ -145,36 +148,8 @@
     pending = []
 
     loads[0].wait()
-    gather_edges(basis, basis_edge := rest[-1])
-    pl.semaphore_wait(barrier, len(greeted))
-    basis_copies = exchange(basis, basis_edge, basis_send, basis_recv)
-    start_exchange(basis_copies)
-
-    row16 = lax.broadcasted_iota(jnp.int32, (kprim, 3 * kprim), 0)
-    col48 = lax.broadcasted_iota(jnp.int32, (kprim, 3 * kprim), 1)
-    pick_high = jnp.logical_or(col48 == row16, col48 == row16 + 2 * kprim).astype(F32).astype(BF16)
-    pick_low = (col48 == row16 + kprim).astype(F32).astype(BF16)
-
-    def make_lift(start, size):
-        high, low = split(basis[pl.ds(start, size)])
-        both = (jnp.dot(high, pick_high, preferred_element_type=F32)
-                + jnp.dot(low, pick_low, preferred_element_type=F32))
-        lift[pl.ds(start, size)] = both.astype(BF16)
-
-    make_lift(main, ncell)
-    row32 = lax.broadcasted_iota(jnp.int32, (2 * kprim, 3 * kprim), 0)
-    col32 = lax.broadcasted_iota(jnp.int32, (2 * kprim, 3 * kprim), 1)
-    flip = (row32 == col32).astype(F32).astype(BF16)
-    lx[pl.ds(ncell, 2 * kprim)] = lax.dot_general(
-        flip, lift[pl.ds(main, ncell)], (((1,), (1,)), ((), ())),
-        preferred_element_type=F32).astype(BF16)
-
-    loads[3].wait()
-    loads[4].wait()
-    eye = (lax.broadcasted_iota(jnp.int32, (la, la), 0) == lax.broadcasted_iota(jnp.int32, (la, la), 1))
-    for r in range(lr):
-        column = jnp.sum(jnp.where(eye, cond[pl.ds(r, 1)], 0.0), axis=1, keepdims=True)
-        diag[pl.ds(r * la, la)] = jnp.broadcast_to(4.0 + column, (la, 128))
+    high, low = split(basis_t[...])
+    lx[pl.ds(ncell, 2 * kprim)] = jnp.concatenate([high, low], axis=0)
 
     def store_split(start, value):
         high, low = split(value)
@@ -202,7 +177,6 @@
         energy = jnp.sum(coarse * weights, axis=0, keepdims=True)
         return jnp.concatenate([high, high, low], axis=0), energy
 
-    step_rows = 2 * lr if total % (2 * lr) == 0 else 16
     loads[1].wait()
 
     def split_rhs(r, carry):
@@ -230,6 +204,32 @@
         acc = lax.fori_loop(0, lr, body, jnp.zeros((8, cols), F32))
         return jnp.sum(acc, axis=0, keepdims=True)
 
+    def make_lift(start, size):
+        lift[pl.ds(start, size)] = basis[pl.ds(start, size)].astype(BF16)
+
+    basis_edge = rest[-1]
+    basis_copies = exchange(basis, basis_edge, basis_send, basis_recv)
+
+    def prepare():
+        row16 = lax.broadcasted_iota(jnp.int32, (kprim, 3 * kprim), 0)
+        col48 = lax.broadcasted_iota(jnp.int32, (kprim, 3 * kprim), 1)
+        pick_high = jnp.logical_or(col48 == row16, col48 == row16 + 2 * kprim).astype(F32).astype(BF16)
+        pick_low = (col48 == row16 + kprim).astype(F32).astype(BF16)
+
+        def turned(half, pick):
+            return lax.dot_general(half, pick, (((0,), (0,)), ((), ())), preferred_element_type=F32)
+        basis[pl.ds(main, ncell)] = turned(high, pick_high) + turned(low, pick_low)
+
+        gather_edges(basis, basis_edge)
+        start_exchange(basis_copies)
+        make_lift(main, ncell)
+
+        loads[3].wait()
+        eye = (lax.broadcasted_iota(jnp.int32, (la, la), 0) == lax.broadcasted_iota(jnp.int32, (la, la), 1))
+        for r in range(lr):
+            column = jnp.sum(jnp.where(eye, cond[pl.ds(r, 1)], 0.0), axis=1, keepdims=True)
+            diag[pl.ds(r * la, la)] = jnp.broadcast_to(4.0 + column, (la, 128))
+
     product = None
     alpha = None
     for k in range(ITERS):
@@ -242,11 +242,19 @@
         edge = edges.at[k]
         gather_edges(ybuf, edge)
         copies = exchange(ybuf, edge, edge_send.at[k], edge_recv.at[k])
-        start_exchange(copies)
+        if k == 0:
+            pl.semaphore_wait(barrier, len(greeted))
         value = jnp.concatenate(
             [coarse, inner, curve, jnp.zeros((6, cols), F32)], axis=0)
-        value = reduce(k, kprim + 8, value)
+
+        def shadow():
+            start_exchange(copies)
+            if k == 0:
+                prepare()
+        value = reduce(k, kprim + 8, value, shadow)
         coarse, inner, curve = value[:kprim], value[kprim:kprim + 1], value[kprim + 1:kprim + 2]
+        if k == 0:
+            loads[4].wait()
         weights, energy = lifted_weights(coarse)
         inner = inner + energy
         if k == 0:
@@ -264,7 +272,7 @@
                 zed[pl.ds(at, step_rows)] = got
                 direction[pl.ds(at, step_rows)] = got
                 return carry
-            lax.fori_loop(0, total // step_rows, begin, 0)
+            lax.fori_loop(0, total // step_rows, begin, 0, unroll=True)
         else:
             alpha = product / curve
             fresh = alpha * alpha * inner - product
@@ -285,7 +293,7 @@
                 direction[pl.ds(at, step_rows)] = fresh_zed + ratio * old
                 return carry
             solution_acc = rest[-2]
-            lax.fori_loop(0, total // step_rows, update, 0)
+            lax.fori_loop(0, total // step_rows, update, 0, unroll=True)
         curve = apply_operator()
     curve = reduce(ITERS, 8, jnp.broadcast_to(curve, (8, cols)))[:1]
     alpha = product / curve
@@ -305,7 +313,7 @@
     first, radices = stage_radices(n_ang)
     sizes = [n_rad * first] + radices
     nst = len(sizes)
-    total = ncell + 2 * la + 2 * lr
+    total = -(-(ncell + 2 * la + 2 * lr) // 256) * 256
     rows = kprim + 8
     dma = pltpu.SemaphoreType.DMA
     scratch = [
@@ -318,7 +326,8 @@
         pltpu.VMEM((ncell, 128), F32),
         pltpu.VMEM((lr, la), F32),
         pltpu.VMEM((kprim, kprim), F32),
-        pltpu.VMEM((total, kprim), F32),
+        pltpu.VMEM((kprim, ncell), F32),
+        pltpu.VMEM((total, 3 * kprim), F32),
         pltpu.VMEM((total, 3 * kprim), BF16),
         pltpu.VMEM((ITERS, total, cols), F32),
         pltpu.VMEM((ITERS, 2, lr, cols), F32),
@@ -328,19 +337,19 @@
     scratch += [dma((5,)), dma((4,)), dma((4,)), dma((ITERS, 4)), dma((ITERS, 4))]
     for s in sizes:
         scratch += [dma((ITERS + 1, s - 1)), dma((ITERS + 1, s - 1))]
-    scratch += [pltpu.VMEM((total, cols), F32), pltpu.VMEM((2, lr, kprim), F32)]
+    scratch += [pltpu.VMEM((total, cols), F32), pltpu.VMEM((2, lr, 3 * kprim), F32)]
     flat = pl.pallas_call(
         functools.partial(kernel, (n_ang, n_rad, lr, la, cols, kprim, first, radices)),
         out_shape=jax.ShapeDtypeStruct((ncell, cols), F32),
-        in_specs=[pl.BlockSpec(memory_space=pl.ANY)] * 5,
+        in_specs=[pl.BlockSpec(memory_space=pltpu.HBM)] * 5,
         out_specs=pl.BlockSpec(memory_space=pltpu.VMEM),
         scratch_shapes=scratch,
         compiler_params=pltpu.CompilerParams(
-            collective_id=0, has_side_effects=True, vmem_limit_bytes=48 * 1024 * 1024),
+            collective_id=0, has_side_effects=True, vmem_limit_bytes=61 * 1024 * 1024),
         cost_estimate=pl.CostEstimate(
             flops=2 * ITERS * ncell * ncell * 2 * cols, bytes_accessed=5 * 1024 * 1024, transcendentals=0),
     )(right_side.reshape(ncell, cols), conduct, local_inverse.reshape(ncell, ncell),
-      primal_basis.reshape(ncell, kprim), coarse_inverse)
+      primal_basis.reshape(ncell, kprim).T, coarse_inverse)
     return flat.reshape(lr, la, cols)
 
 

time: 69.7 us -> 52.9 us (0.76)
  Pallas kernels: 63.1 us -> 50.5 us
  local copies, waits for them, and re-layouts: 6.21 us -> 2.29 us
    pallas_call x1, Pallas kernels: 63.1 us -> 50.5 us  [per_device(): pl.pallas_call(functools.partial(kernel, (n_ang, n_rad, lr, la, cols, kpr...]
    unnamed x10 -> x1, local copies, waits for them, and re-layouts: 6.21 us -> 2.29 us
where the time goes in v2:
time: 52.9 us; the launch traced here: 52.8 us
  Pallas kernels  50.5 us (95%)
  local copies, waits for them, and re-layouts  2.29 us (4%)
    pallas_call x1, Pallas kernels, per_device(): pl.pallas_call(functools.partial(kernel, (n_ang, n_rad, lr, la, cols, kpr...  50.5 us
    unnamed x1, local copies, waits for them, and re-layouts  2.29 us

profile of v2, /device:TPU:0, one launch (start us, length us, event | category | flops | bytes accessed | tf_op | source)
XLA Modules:
  0.0 52.8 jit_solution(4464553567342361496)
XLA Ops:
  0.0 50.5 %shard_map.55 = f32[1024,256]{1,0:T(8,128)} custom-call(f32[1024,256]{1,0:T(8,128)} %bitcast.8, f32[16,64]{1,0:T(8,128)} %cond_hbm.1, bf16[1024,1024]{1,0:T(8,128)(2,1)} %bitcast.7, f32[16,1024]{1,0:T(8,128)} %bitcast.9, f32[16,16]{1,0:T(8,128)} %coarse_hbm.1), custom_call_target="tpu_custom_call" | custom-call | flops 3221225472 | bytes 5242880 | tf_op jit(solution)/shard_map/pallas_call | solution.py:341
  50.5 2.3 %copy.7 = f32[16,64,256]{2,1,0:T(8,128)} copy(f32[16,64,256]{2,1,0:T(8,128)} %bitcast.6) | data formatting | bytes 2097152

commit v3 on v2

--- a/solution.py
+++ b/solution.py
@@ -74,8 +74,8 @@
                 found.append((ang + (other - digit) * stride, rad))
         return found
 
-    basis[pl.ds(0, la)] = jnp.zeros((la, 3 * kprim), F32)
-    basis[pl.ds(bottom, total - bottom)] = jnp.zeros((total - bottom, 3 * kprim), F32)
+    basis[pl.ds(0, la)] = jnp.zeros((la, 128), F32)
+    basis[pl.ds(bottom, total - bottom)] = jnp.zeros((total - bottom, 128), F32)
     for k in range(ITERS):
         ybufs[k, pl.ds(0, la)] = jnp.zeros((la, cols), F32)
         ybufs[k, pl.ds(bottom, total - bottom)] = jnp.zeros((total - bottom, cols), F32)
@@ -146,6 +146,22 @@
         return value
 
     pending = []
+    groups_of = cols // 128
+
+    def fold(*values):
+        pieces = [v[:, g * 128:(g + 1) * 128] for v in values for g in range(groups_of)]
+        spare = -sum(p.shape[0] for p in pieces) % 8
+        if spare:
+            pieces.append(jnp.zeros((spare, 128), F32))
+        return jnp.concatenate(pieces, axis=0)
+
+    def unfold(value, *counts):
+        found, at = [], 0
+        for count in counts:
+            found.append(jnp.concatenate(
+                [value[at + g * count:at + (g + 1) * count] for g in range(groups_of)], axis=1))
+            at += groups_of * count
+        return found
 
     loads[0].wait()
     high, low = split(basis_t[...])
@@ -205,14 +221,14 @@
         return jnp.sum(acc, axis=0, keepdims=True)
 
     def make_lift(start, size):
-        lift[pl.ds(start, size)] = basis[pl.ds(start, size)].astype(BF16)
+        lift[pl.ds(start, size)] = basis[pl.ds(start, size), pl.ds(0, 3 * kprim)].astype(BF16)
 
     basis_edge = rest[-1]
     basis_copies = exchange(basis, basis_edge, basis_send, basis_recv)
 
     def prepare():
-        row16 = lax.broadcasted_iota(jnp.int32, (kprim, 3 * kprim), 0)
-        col48 = lax.broadcasted_iota(jnp.int32, (kprim, 3 * kprim), 1)
+        row16 = lax.broadcasted_iota(jnp.int32, (kprim, 128), 0)
+        col48 = lax.broadcasted_iota(jnp.int32, (kprim, 128), 1)
         pick_high = jnp.logical_or(col48 == row16, col48 == row16 + 2 * kprim).astype(F32).astype(BF16)
         pick_low = (col48 == row16 + kprim).astype(F32).astype(BF16)
 
@@ -244,15 +260,14 @@
         copies = exchange(ybuf, edge, edge_send.at[k], edge_recv.at[k])
         if k == 0:
             pl.semaphore_wait(barrier, len(greeted))
-        value = jnp.concatenate(
-            [coarse, inner, curve, jnp.zeros((6, cols), F32)], axis=0)
+        value = fold(coarse, inner, curve)
 
         def shadow():
             start_exchange(copies)
             if k == 0:
                 prepare()
-        value = reduce(k, kprim + 8, value, shadow)
-        coarse, inner, curve = value[:kprim], value[kprim:kprim + 1], value[kprim + 1:kprim + 2]
+        value = reduce(k, value.shape[0], value, shadow)
+        coarse, inner, curve = unfold(value, kprim, 1, 1)
         if k == 0:
             loads[4].wait()
         weights, energy = lifted_weights(coarse)
@@ -295,7 +310,8 @@
             solution_acc = rest[-2]
             lax.fori_loop(0, total // step_rows, update, 0, unroll=True)
         curve = apply_operator()
-    curve = reduce(ITERS, 8, jnp.broadcast_to(curve, (8, cols)))[:1]
+    value = fold(curve)
+    curve, = unfold(reduce(ITERS, value.shape[0], value), 1)
     alpha = product / curve
 
     def finish(r, carry):
@@ -314,7 +330,7 @@
     sizes = [n_rad * first] + radices
     nst = len(sizes)
     total = -(-(ncell + 2 * la + 2 * lr) // 256) * 256
-    rows = kprim + 8
+    rows = -(-(kprim + 2) * (cols // 128) // 8) * 8
     dma = pltpu.SemaphoreType.DMA
     scratch = [
         pltpu.VMEM((ncell + 2 * kprim, ncell), BF16),
@@ -327,17 +343,17 @@
         pltpu.VMEM((lr, la), F32),
         pltpu.VMEM((kprim, kprim), F32),
         pltpu.VMEM((kprim, ncell), F32),
-        pltpu.VMEM((total, 3 * kprim), F32),
+        pltpu.VMEM((total, 128), F32),
         pltpu.VMEM((total, 3 * kprim), BF16),
         pltpu.VMEM((ITERS, total, cols), F32),
         pltpu.VMEM((ITERS, 2, lr, cols), F32),
-        pltpu.VMEM((ITERS + 1, nst, rows, cols), F32),
+        pltpu.VMEM((ITERS + 1, nst, rows, 128), F32),
     ]
-    scratch += [pltpu.VMEM((ITERS + 1, s - 1, rows, cols), F32) for s in sizes]
+    scratch += [pltpu.VMEM((ITERS + 1, s - 1, rows, 128), F32) for s in sizes]
     scratch += [dma((5,)), dma((4,)), dma((4,)), dma((ITERS, 4)), dma((ITERS, 4))]
     for s in sizes:
         scratch += [dma((ITERS + 1, s - 1)), dma((ITERS + 1, s - 1))]
-    scratch += [pltpu.VMEM((total, cols), F32), pltpu.VMEM((2, lr, 3 * kprim), F32)]
+    scratch += [pltpu.VMEM((total, cols), F32), pltpu.VMEM((2, lr, 128), F32)]
     flat = pl.pallas_call(
         functools.partial(kernel, (n_ang, n_rad, lr, la, cols, kprim, first, radices)),
         out_shape=jax.ShapeDtypeStruct((ncell, cols), F32),

time: 52.9 us -> 50.6 us (0.957)
  Pallas kernels: 50.5 us -> 48.2 us
    pallas_call x1, Pallas kernels: 50.5 us -> 48.2 us  [per_device(): pl.pallas_call(functools.partial(kernel, (n_ang, n_rad, lr, la, cols, kpr...]
where the time goes in v3:
time: 50.6 us; the launch traced here: 50.5 us
  Pallas kernels  48.2 us (95%)
  local copies, waits for them, and re-layouts  2.29 us (5%)
    pallas_call x1, Pallas kernels, per_device(): pl.pallas_call(functools.partial(kernel, (n_ang, n_rad, lr, la, cols, kpr...  48.2 us
    unnamed x1, local copies, waits for them, and re-layouts  2.29 us

profile of v3, /device:TPU:0, one launch (start us, length us, event | category | flops | bytes accessed | tf_op | source)
XLA Modules:
  0.0 50.5 jit_solution(4989358095083107325)
XLA Ops:
  0.0 48.2 %shard_map.55 = f32[1024,256]{1,0:T(8,128)} custom-call(f32[1024,256]{1,0:T(8,128)} %bitcast.8, f32[16,64]{1,0:T(8,128)} %cond_hbm.1, bf16[1024,1024]{1,0:T(8,128)(2,1)} %bitcast.7, f32[16,1024]{1,0:T(8,128)} %bitcast.9, f32[16,16]{1,0:T(8,128)} %coarse_hbm.1), custom_call_target="tpu_custom_call" | custom-call | flops 3221225472 | bytes 5242880 | tf_op jit(solution)/shard_map/pallas_call | solution.py:357
  48.2 2.3 %copy.7 = f32[16,64,256]{2,1,0:T(8,128)} copy(f32[16,64,256]{2,1,0:T(8,128)} %bitcast.6) | data formatting | bytes 2097152

commit v4 on v3

--- a/solution.py
+++ b/solution.py
@@ -226,7 +226,7 @@
     basis_edge = rest[-1]
     basis_copies = exchange(basis, basis_edge, basis_send, basis_recv)
 
-    def prepare():
+    def send_basis():
         row16 = lax.broadcasted_iota(jnp.int32, (kprim, 128), 0)
         col48 = lax.broadcasted_iota(jnp.int32, (kprim, 128), 1)
         pick_high = jnp.logical_or(col48 == row16, col48 == row16 + 2 * kprim).astype(F32).astype(BF16)
@@ -238,8 +238,9 @@
 
         gather_edges(basis, basis_edge)
         start_exchange(basis_copies)
+
+    def prepare():
         make_lift(main, ncell)
-
         loads[3].wait()
         eye = (lax.broadcasted_iota(jnp.int32, (la, la), 0) == lax.broadcasted_iota(jnp.int32, (la, la), 1))
         for r in range(lr):
@@ -251,6 +252,8 @@
     for k in range(ITERS):
         ybuf = ybufs.at[k]
         if k == 0:
+            pl.semaphore_wait(barrier, len(greeted))
+            send_basis()
             inner, coarse = apply_local(rhs, ybuf)
             curve = jnp.zeros((1, cols), F32)
         else:
@@ -258,8 +261,6 @@
         edge = edges.at[k]
         gather_edges(ybuf, edge)
         copies = exchange(ybuf, edge, edge_send.at[k], edge_recv.at[k])
-        if k == 0:
-            pl.semaphore_wait(barrier, len(greeted))
         value = fold(coarse, inner, curve)
 
         def shadow():
@@ -314,11 +315,17 @@
     curve, = unfold(reduce(ITERS, value.shape[0], value), 1)
     alpha = product / curve
 
-    def finish(r, carry):
-        at = pl.multiple_of(r * la, la)
-        out_ref[pl.ds(at, la)] = solution_acc[pl.ds(at + la, la)] + alpha * direction[pl.ds(at + la, la)]
-        return carry
-    lax.fori_loop(0, lr, finish, 0)
+    part = ncell // 4
+    stores = []
+    for i in range(4):
+        at = i * part
+        solution_acc[pl.ds(at + la, part)] = (
+            solution_acc[pl.ds(at + la, part)] + alpha * direction[pl.ds(at + la, part)])
+        stores.append(pltpu.make_async_copy(
+            solution_acc.at[pl.ds(at + la, part)], out_ref.at[pl.ds(at, part)], load_sem.at[5 + i]))
+        stores[-1].start()
+    for store in stores:
+        store.wait()
     for copy in pending:
         copy.wait_send()
 
@@ -350,7 +357,7 @@
         pltpu.VMEM((ITERS + 1, nst, rows, 128), F32),
     ]
     scratch += [pltpu.VMEM((ITERS + 1, s - 1, rows, 128), F32) for s in sizes]
-    scratch += [dma((5,)), dma((4,)), dma((4,)), dma((ITERS, 4)), dma((ITERS, 4))]
+    scratch += [dma((9,)), dma((4,)), dma((4,)), dma((ITERS, 4)), dma((ITERS, 4))]
     for s in sizes:
         scratch += [dma((ITERS + 1, s - 1)), dma((ITERS + 1, s - 1))]
     scratch += [pltpu.VMEM((total, cols), F32), pltpu.VMEM((2, lr, 128), F32)]
@@ -358,7 +365,7 @@
         functools.partial(kernel, (n_ang, n_rad, lr, la, cols, kprim, first, radices)),
         out_shape=jax.ShapeDtypeStruct((ncell, cols), F32),
         in_specs=[pl.BlockSpec(memory_space=pltpu.HBM)] * 5,
-        out_specs=pl.BlockSpec(memory_space=pltpu.VMEM),
+        out_specs=pl.BlockSpec(memory_space=pltpu.HBM),
         scratch_shapes=scratch,
         compiler_params=pltpu.CompilerParams(
             collective_id=0, has_side_effects=True, vmem_limit_bytes=61 * 1024 * 1024),

time: 50.6 us -> 51.6 us (1.020)
  Pallas kernels: 48.2 us -> 49.1 us
    pallas_call x1, Pallas kernels: 48.2 us -> 49.1 us  [per_device(): pl.pallas_call(functools.partial(kernel, (n_ang, n_rad, lr, la, cols, kpr...]
where the time goes in v4:
time: 51.6 us; the launch traced here: 51.4 us
  Pallas kernels  49.1 us (95%)
  local copies, waits for them, and re-layouts  2.29 us (4%)
    pallas_call x1, Pallas kernels, per_device(): pl.pallas_call(functools.partial(kernel, (n_ang, n_rad, lr, la, cols, kpr...  49.1 us
    unnamed x1, local copies, waits for them, and re-layouts  2.29 us

profile of v4, /device:TPU:0, one launch (start us, length us, event | category | flops | bytes accessed | tf_op | source)
XLA Modules:
  0.0 51.4 jit_solution(13649841110051170724)
XLA Ops:
  0.0 49.1 %shard_map.55 = f32[1024,256]{1,0:T(8,128)} custom-call(f32[1024,256]{1,0:T(8,128)} %bitcast.8, f32[16,64]{1,0:T(8,128)} %cond_hbm.1, bf16[1024,1024]{1,0:T(8,128)(2,1)} %bitcast.7, f32[16,1024]{1,0:T(8,128)} %bitcast.9, f32[16,16]{1,0:T(8,128)} %coarse_hbm.1), custom_call_target="tpu_custom_call" | custom-call | flops 3221225472 | bytes 5242880 | tf_op jit(solution)/shard_map/pallas_call | solution.py:364
  49.1 2.3 %copy.7 = f32[16,64,256]{2,1,0:T(8,128)} copy(f32[16,64,256]{2,1,0:T(8,128)} %bitcast.6) | data formatting | bytes 2097152

commit v5 on v3

--- a/solution.py
+++ b/solution.py
@@ -182,7 +182,7 @@
             out[pl.ds(main + start, tile)] = got
             part = got * vec[pl.ds(start, tile)]
             return acc + jnp.sum(part.reshape(tile // 8, 8, cols), axis=0)
-        acc = lax.fori_loop(0, ncell // tile, body, jnp.zeros((8, cols), F32))
+        acc = lax.fori_loop(0, ncell // tile, body, jnp.zeros((8, cols), F32), unroll=True)
         small = jnp.dot(lx[pl.ds(ncell, 2 * kprim)], right[...], preferred_element_type=F32)
         both = small[:, :cols] + small[:, cols:]
         return jnp.sum(acc, axis=0, keepdims=True), both[:kprim] + both[kprim:]
@@ -217,7 +217,7 @@
             image[pl.ds(at, la)] = got
             store_split(at, got)
             return acc + jnp.sum((got * here).reshape(la // 8, 8, cols), axis=0)
-        acc = lax.fori_loop(0, lr, body, jnp.zeros((8, cols), F32))
+        acc = lax.fori_loop(0, lr, body, jnp.zeros((8, cols), F32), unroll=4)
         return jnp.sum(acc, axis=0, keepdims=True)
 
     def make_lift(start, size):

time: 50.6 us -> 48.8 us (0.964)
  Pallas kernels: 48.2 us -> 46.3 us
    pallas_call x1, Pallas kernels: 48.2 us -> 46.3 us  [per_device(): pl.pallas_call(functools.partial(kernel, (n_ang, n_rad, lr, la, cols, kpr...]
where the time goes in v5:
time: 48.8 us; the launch traced here: 48.6 us
  Pallas kernels  46.3 us (95%)
  local copies, waits for them, and re-layouts  2.29 us (5%)
    pallas_call x1, Pallas kernels, per_device(): pl.pallas_call(functools.partial(kernel, (n_ang, n_rad, lr, la, cols, kpr...  46.3 us
    unnamed x1, local copies, waits for them, and re-layouts  2.29 us

profile of v5, /device:TPU:0, one launch (start us, length us, event | category | flops | bytes accessed | tf_op | source)
XLA Modules:
  0.0 48.6 jit_solution(15382985764818256837)
XLA Ops:
  0.0 46.3 %shard_map.55 = f32[1024,256]{1,0:T(8,128)} custom-call(f32[1024,256]{1,0:T(8,128)} %bitcast.8, f32[16,64]{1,0:T(8,128)} %cond_hbm.1, bf16[1024,1024]{1,0:T(8,128)(2,1)} %bitcast.7, f32[16,1024]{1,0:T(8,128)} %bitcast.9, f32[16,16]{1,0:T(8,128)} %coarse_hbm.1), custom_call_target="tpu_custom_call" | custom-call | flops 3221225472 | bytes 5242880 | tf_op jit(solution)/shard_map/pallas_call | solution.py:357
  46.3 2.3 %copy.7 = f32[16,64,256]{2,1,0:T(8,128)} copy(f32[16,64,256]{2,1,0:T(8,128)} %bitcast.6) | data formatting | bytes 2097152
